TPU v7x, 256 devices: a whole 4x4x8 slice. The times are simulated.
256 devices in a mesh: tile: 16 (over z, core), lev: 4 (over x), tag: 4 (over y).
Axes of the slice: x: 4, y: 4, z: 8, core: 2. Of those that a mesh axis runs over, the one named last changes fastest.
Arguments:
- parent_field: float32 [8, 32, 256, 1024], P('tag', 'lev', 'tile'), may hold values from -6 to 6
- nest_field: float32 [8, 32, 256, 1024], P('tag', 'lev', 'tile'), may hold values from -6 to 6
- parent_mixing: float32 [32, 256, 1024], P('lev', 'tile'), may hold values from 0.05 to 5
- parent_eastward: float32 [256, 1024], P('tile'), may hold values from 0.02 to 0.12
- parent_northward: float32 [256, 1024], P('tile'), may hold values from 0.02 to 0.12
- nest_eastward: float32 [256, 1024], P('tile'), may hold values from 0.02 to 0.12
- nest_northward: float32 [256, 1024], P('tile'), may hold values from 0.02 to 0.12
- strip_tile: int32 [16, 256], replicated, may hold values from 0 to 15, as said below
- strip_block: int32 [16, 256], replicated, may hold values from 0 to 127
- strip_target: int32 [16, 256], replicated, may hold values from 0 to 127
- strip_count: int32 [16], replicated, may hold values from 1 to 256, as said below
Outputs:
- parent_adjoint: float32 [8, 32, 256, 1024], P('tag', 'lev', 'tile')
- nest_adjoint: float32 [8, 32, 256, 1024], P('tag', 'lev', 'tile')
- bulk_adjoint: float32 [32, 256, 1024], P('lev', 'tile', 'tag')
Inputs may be any that keep to these rules, and one draw needn't show every extreme that they name: `strip_tile`: among the first strip_count[j] entries of row j, every parent tile appears at most 16 times; in the row whose count is 256 every parent tile appears exactly 16 times. `strip_count`: exactly one nest tile lists 256 strips; every other lists at most 128.
All inputs are finite; a program needn't handle non-finite values.
Results may differ from a plain program's by a relative error of at most 0.0003.
Values sent between devices are 32-bit elements; how exact they have to be, the bound alone decides.
A program may use at most 64 MiB of HBM per device.

v0:
```python
import jax
import jax.numpy as jnp
from jax import lax
from jax.sharding import PartitionSpec as P

CAP = 16
NSUB = 3
HIGHEST = lax.Precision.HIGHEST


def extended(cells, sides, width):
    for axis, dim in sides:
        count = lax.axis_size(axis)
        ends = count - 1
        head = lax.slice_in_dim(cells, 0, width, axis=dim)
        tail = lax.slice_in_dim(cells, cells.shape[dim] - width, cells.shape[dim], axis=dim)
        cells = jnp.concatenate(
            [
                lax.ppermute(tail, axis, [(i, (i + 1) % count) for i in range(ends)]),
                cells,
                lax.ppermute(head, axis, [((i + 1) % count, i) for i in range(ends)]),
            ],
            axis=dim,
        )
    return cells


def tridiagonal(source, mixing):
    level_count = mixing.shape[0]
    mixing_up = jnp.concatenate([mixing[1:], jnp.zeros_like(mixing[:1])], axis=0)
    diagonal = 1.0 + mixing + mixing_up
    ratio_now = jnp.zeros_like(mixing[0])
    carry_now = jnp.zeros_like(source[:, 0])
    ratios = []
    carries = []
    for lev_index in range(level_count):
        pivot_now = diagonal[lev_index] + mixing[lev_index] * ratio_now
        ratio_now = -mixing_up[lev_index] / pivot_now
        carry_now = (source[:, lev_index] + mixing[lev_index] * carry_now) / pivot_now
        ratios.append(ratio_now)
        carries.append(carry_now)
    value_now = carries[level_count - 1]
    results = [value_now]
    for lev_index in range(level_count - 2, -1, -1):
        value_now = carries[lev_index] - ratios[lev_index] * value_now
        results.append(value_now)
    return jnp.stack(results[::-1], axis=1)


def relax(padded, eastward):
    center = padded[:-1, 1:-1]
    row_above = padded[:-1, :-2]
    row_below = padded[:-1, 2:]
    north_here = padded[-1, 1:-1]
    north_above = padded[-1, :-2]
    zero_column = jnp.zeros_like(center[:, :, :1])
    east_cell = jnp.concatenate([center[:, :, 1:], zero_column], axis=2)
    west_cell = jnp.concatenate([zero_column, center[:, :, :-1]], axis=2)
    west_rate = jnp.concatenate([jnp.zeros_like(eastward[:, :1]), eastward[:, :-1]], axis=1)
    return (
        center
        + north_here * (row_below - center)
        + north_above * (row_above - center)
        + eastward * (east_cell - center)
        + west_rate * (west_cell - center)
    )


def rims(stacked):
    return extended(stacked, (("tile", 1),), 1)


def advance(start, solved, parent_eastward, parent_northward, nest_eastward, nest_northward):
    tag_count, level_count, row_count, col_count = start.shape
    line_count = tag_count * level_count
    nest_now = start.reshape(line_count, row_count, col_count)
    parent_now = solved.reshape(line_count, row_count, col_count)
    for sub_step in range(NSUB):
        nest_stack = jnp.concatenate([nest_now, nest_northward[None]], axis=0)
        if sub_step == 0:
            parent_stack = jnp.concatenate([parent_now, parent_northward[None]], axis=0)
            padded = rims(jnp.concatenate([parent_stack, nest_stack], axis=0))
            parent_now = relax(padded[: line_count + 1], parent_eastward)
            nest_now = relax(padded[line_count + 1 :], nest_eastward)
        else:
            nest_now = relax(rims(nest_stack), nest_eastward)
    full_shape = (tag_count, level_count, row_count, col_count)
    return (parent_now.reshape(full_shape), nest_now.reshape(full_shape))


def deliver(parent_field, strip_tile, strip_block, strip_target, strip_count):
    tag_count, level_count, row_count, col_count = parent_field.shape
    line_count = tag_count * level_count
    block_count = row_count * col_count // 128
    tile_count, slot_total = strip_tile.shape
    own_index = lax.axis_index("tile")
    positions = jnp.arange(slot_total, dtype=jnp.int32)
    is_live = positions[None, :] < strip_count[:, None]
    from_here = jnp.logical_and(is_live, strip_tile == own_index).astype(jnp.int32)
    slot_rank = jnp.cumsum(from_here, axis=1) - 1
    slot_index = jnp.arange(CAP, dtype=jnp.int32)
    select = from_here[:, None, :] * (slot_rank[:, None, :] == slot_index[None, :, None]).astype(
        jnp.int32
    )
    source_block = jnp.sum(select * strip_block[:, None, :], axis=2).reshape(-1)
    filled = jnp.sum(select, axis=2).reshape(-1).astype(jnp.float32)
    blocks = parent_field.reshape(line_count, block_count, 128)
    packed = jnp.take(blocks, source_block, axis=1) * filled[None, :, None]
    received = lax.all_to_all(packed, "tile", split_axis=1, concat_axis=1, tiled=True)
    own_tile = lax.dynamic_index_in_dim(strip_tile, own_index, 0, keepdims=False)
    own_target = lax.dynamic_index_in_dim(strip_target, own_index, 0, keepdims=False)
    own_count = lax.dynamic_index_in_dim(strip_count, own_index, 0, keepdims=False)
    own_live = (positions < own_count).astype(jnp.int32)
    from_source = (own_tile[:, None] == jnp.arange(tile_count, dtype=jnp.int32)[None, :]).astype(
        jnp.int32
    ) * own_live[:, None]
    own_rank = jnp.sum((jnp.cumsum(from_source, axis=0) - 1) * from_source, axis=1)
    arrival = own_tile * CAP + own_rank
    pick_slot = (arrival[:, None] == jnp.arange(tile_count * CAP, dtype=jnp.int32)[None, :]).astype(
        jnp.float32
    )
    pick_slot = pick_slot * own_live[:, None].astype(jnp.float32)
    place_block = (own_target[:, None] == jnp.arange(block_count, dtype=jnp.int32)[None, :]).astype(
        jnp.float32
    )
    routing = jnp.dot(pick_slot.T, place_block, precision=HIGHEST)
    forcing = jnp.einsum("lic,ib->lbc", received, routing, precision=HIGHEST)
    return forcing.reshape(tag_count, level_count, row_count, col_count)


def shards(
    parent_field,
    nest_field,
    parent_mixing,
    parent_eastward,
    parent_northward,
    nest_eastward,
    nest_northward,
    strip_tile,
    strip_block,
    strip_target,
    strip_count,
):
    tag_count = parent_field.shape[0]
    forcing = deliver(parent_field, strip_tile, strip_block, strip_target, strip_count)
    stacked = jnp.concatenate([parent_field, parent_mixing[None]], axis=0)
    columns = lax.all_to_all(stacked, "lev", split_axis=3, concat_axis=1, tiled=True)
    column_result = tridiagonal(columns[:tag_count], columns[tag_count])
    solved = lax.all_to_all(column_result, "lev", split_axis=1, concat_axis=3, tiled=True)
    parent_adjoint, nest_adjoint = advance(
        nest_field + forcing,
        solved,
        parent_eastward,
        parent_northward,
        nest_eastward,
        nest_northward,
    )
    bulk_adjoint = lax.psum_scatter(
        jnp.sum(parent_adjoint, axis=0), "tag", scatter_dimension=2, tiled=True
    )
    return (parent_adjoint, nest_adjoint, bulk_adjoint)


def solution(mesh):
    in_specs = (
        P("tag", "lev", "tile", None),
        P("tag", "lev", "tile", None),
        P("lev", "tile", None),
        P("tile", None),
        P("tile", None),
        P("tile", None),
        P("tile", None),
        P(),
        P(),
        P(),
        P(),
    )
    out_specs = (
        P("tag", "lev", "tile", None),
        P("tag", "lev", "tile", None),
        P("lev", "tile", "tag"),
    )
    return jax.shard_map(shards, mesh=mesh, in_specs=in_specs, out_specs=out_specs, check_vma=False)
```

profile of v0, /device:TPU:2, one launch (start us, length us, event | category | flops | bytes accessed | tf_op | source)
XLA Modules:
  0.0 209.8 jit_solution(3081090923372214536)
XLA Ops:
  7.2 1.5 pad_maximum_fusion.5
  8.7 6.9 %copy.55 = f32[3,8,16,1024]{2,1,0,3:T(8,128)} copy(f32[3,8,16,1024]{3,2,1,0:T(8,128)S(1)} %pad_maximum_fusion.5) | data formatting | bytes 3145728 | tf_op jit(solution)/shard_map/concatenate | solution.py:146
  15.6 8.3 %reshape.176 = f32[4,1,98304]{2,1,0:T(1,128)} reshape(f32[1024,3,8,16]{3,2,1,0:T(8,128)} %bitcast.230) | data formatting | bytes 3145728
  23.9 5.9 %all-to-all-start = ((f32[4,1,98304]{2,1,0:T(1,128)}), f32[4,1,98304]{2,1,0:T(1,128)S(1)}, u32[]{:S(2)}, u32[]{:S(2)}) async-start(f32[4,1,98304]{2,1,0:T(1,128)} %reshape.176), calls=%async_computation | async-start | bytes 3145728 | tf_op jit(solution)/shard_map/all_to_all | solution.py:147
  29.8 1.1 reshape.159
  31.0 0.6 reduce-window.16
  32.0 0.6 select_reduce_fusion
  32.7 1.8 copy.65
  34.7 13.4 %all-to-all-done = f32[4,1,98304]{2,1,0:T(1,128)S(1)} async-done(((f32[4,1,98304]{2,1,0:T(1,128)}), f32[4,1,98304]{2,1,0:T(1,128)S(1)}, u32[]{:S(2)}, u32[]{:S(2)}) %all-to-all-start) | async-done | bytes 1572896 | tf_op jit(solution)/shard_map/all_to_all | solution.py:147
  48.1 1.2 copy-done.1
  49.2 0.5 broadcast.2764
  49.8 6.2 %reduce.4 = f32[4,98304]{1,0:T(4,128)S(1)} reduce(f32[4,1,98304]{2,1,0:T(1,128)} %copy-done.1, f32[]{:T(128)} %broadcast.2764), dimensions={1}, to_apply=%all_to_all.25.reduce_sub_computation | reduce | bytes 3145732 | tf_op jit(solution)/shard_map/all_to_all | solution.py:147
  55.9 8.9 %reshape.177 = f32[1024,3,8,16]{3,2,1,0:T(8,128)} reshape(f32[4,98304]{1,0:T(4,128)S(1)} %reduce.4) | data formatting | bytes 3145728
  64.8 7.8 %copy.69 = f32[3,8,16,4,256]{4,3,2,1,0:T(4,128)S(1)} copy(f32[3,8,16,4,256]{2,1,0,4,3:T(8,128)} %bitcast.231) | data formatting | bytes 3145728 | tf_op jit(solution)/shard_map/all_to_all | solution.py:147
  74.9 1.0 copy.59
  75.9 5.7 %all-to-all-start.1 = ((f32[2,32,16,256]{3,2,0,1:T(8,128)}), f32[2,32,16,256]{3,2,0,1:T(8,128)}, u32[]{:S(2)}, u32[]{:S(2)}) async-start(f32[2,32,16,256]{3,2,0,1:T(8,128)} %copy.59), calls=%async_computation.1 | async-start | bytes 2097152 | tf_op jit(solution)/shard_map/all_to_all | solution.py:149
  81.6 1.0 gather_fusion
  82.6 2.5 %multiply_bitcast_fusion = f32[16,256,128]{2,0,1:T(8,128)} fusion(f32[256,16,128]{2,1,0:T(8,128)S(1)} %gather_fusion, f32[256]{0:T(256)S(1)} %convert_element_type.43, pred[256]{0:T(512)(128)(4,1)S(1)} %compare_and_fusion), kind=kLoop, calls=%fused_computation.5 | loop fusion | flops 1048576 | bytes 4195584 | tf_op jit(solution)/shard_map/mul | solution.py:108
  85.2 8.3 %all-to-all-done.1 = f32[2,32,16,256]{3,2,0,1:T(8,128)} async-done(((f32[2,32,16,256]{3,2,0,1:T(8,128)}), f32[2,32,16,256]{3,2,0,1:T(8,128)}, u32[]{:S(2)}, u32[]{:S(2)}) %all-to-all-start.1) | async-done | bytes 1048608 | tf_op jit(solution)/shard_map/all_to_all | solution.py:149
  93.4 9.6 %all-to-all-start.2 = ((f32[16,256,128]{2,0,1:T(8,128)}), f32[16,256,128]{2,0,1:T(8,128)}, u32[]{:S(2)}, u32[]{:S(2)}) async-start(f32[16,256,128]{2,0,1:T(8,128)} %multiply_bitcast_fusion), calls=%async_computation.2 | async-start | bytes 4194304 | tf_op jit(solution)/shard_map/all_to_all | solution.py:109
  103.1 0.6 dynamic_slice.12
  103.7 0.7 compare_convert_fusion.1
  104.3 0.7 constant_dynamic-slice_fusion
  105.1 0.6 reduce-window.14
  106.0 0.7 compare_convert_fusion
  106.7 0.7 fusion.86
  107.9 1.9 copy.61
  109.8 0.5 reshape.154
  110.4 1.7 fusion.137
  112.1 40.2 %all-to-all-done.2 = f32[16,256,128]{2,0,1:T(8,128)} async-done(((f32[16,256,128]{2,0,1:T(8,128)}), f32[16,256,128]{2,0,1:T(8,128)}, u32[]{:S(2)}, u32[]{:S(2)}) %all-to-all-start.2) | async-done | bytes 2097184 | tf_op jit(solution)/shard_map/all_to_all | solution.py:109
  152.3 3.4 %fusion.4 = f32[16,128,128]{2,1,0:T(8,128)S(1)} fusion(f32[256,128,1]{0,1,2:T(8,128)S(1)} %convolution_bitcast_fusion, f32[16,256,128]{2,0,1:T(8,128)} %all-to-all-done.2), kind=kOutput, calls=%fused_computation.12 | convolution fusion | flops 805306368 | bytes 3276800 | tf_op jit(solution)/shard_map/lic,ib->lbc/dot_general | solution.py:127
  155.9 1.4 add.2442
  157.5 2.1 collective-permute-start.1
  159.6 1.3 collective-permute-start
  161.3 1.5 collective-permute-done
  162.9 0.7 fusion.13
  163.6 1.7 fusion.135
  165.4 5.2 %collective-permute-start.3 = (f32[17,1,1024]{2,1,0:T(1,128)S(1)}, f32[17,1,1024]{2,1,0:T(1,128)S(1)}, u32[]{:S(2)}, u32[]{:S(2)}) collective-permute-start(f32[17,1,1024]{2,1,0:T(1,128)S(1)} %get-tuple-element.88), channel_id=1, source_target_pairs={{0,16},{16,32},{32,48},{48,64},{64,80},{80,96},{96,112},{112,128},... | collective-permute-start | bytes 208904 | tf_op jit(solution)/shard_map/ppermute | solution.py:19
  170.7 1.5 collective-permute-start.2
  172.2 1.7 fusion.35
  173.9 2.1 %reduce_sum.39 = f32[8,16,1024]{2,1,0:T(8,128)} reduce(f32[2,8,16,1024]{3,2,1,0:T(8,128)} %bitcast.265, f32[]{:T(128)} %constant.48.clone.1), dimensions={0}, to_apply=%region_7.8 | reduce | flops 131072 | bytes 1572868 | tf_op jit(solution)/shard_map/reduce_sum | solution.py:159
  176.4 0.9 copy-done.3
  177.6 0.6 fusion.20
  178.4 3.0 %collective-permute-start.5 = (f32[17,1,1024]{2,1,0:T(1,128)S(1)}, f32[17,1,1024]{2,1,0:T(1,128)S(1)}, u32[]{:S(2)}, u32[]{:S(2)}) collective-permute-start(f32[17,1,1024]{2,1,0:T(1,128)S(1)} %get-tuple-element.86), channel_id=1, source_target_pairs={{0,16},{16,32},{32,48},{48,64},{64,80},{80,96},{96,112},{112,128},... | collective-permute-start | bytes 208904 | tf_op jit(solution)/shard_map/ppermute | solution.py:19
  181.8 1.3 collective-permute-start.4
  183.4 2.3 %collective-permute-done.4 = f32[17,1,1024]{2,1,0:T(1,128)S(1)} collective-permute-done((f32[17,1,1024]{2,1,0:T(1,128)S(1)}, f32[17,1,1024]{2,1,0:T(1,128)S(1)}, u32[]{:S(2)}, u32[]{:S(2)}) %collective-permute-start.4) | collective-permute-done | bytes 69664 | tf_op jit(solution)/shard_map/ppermute | solution.py:21
  185.7 1.6 fusion.27
  187.3 15.6 %reduce-scatter.2.cloned.1.call-done = f32[8,16,256]{2,1,0:T(8,128)} async-done(((f32[8,16,1024]{2,1,0:T(8,128)}), f32[8,16,256]{2,1,0:T(8,128)}) %reduce-scatter.2.cloned.1.call-update) | async-done | bytes 131088 | tf_op jit(solution)/shard_map/reduce_scatter | solution.py:158
  (118 shorter events, 5.8 us)
Async XLA Ops:
  23.9 5.9 %copy-start.2 = (f32[2,8,16,1024]{3,2,1,0:T(8,128)S(1)}, f32[2,8,16,1024]{3,2,1,0:T(8,128)}, u32[]{:S(2)}) copy-start(f32[2,8,16,1024]{3,2,1,0:T(8,128)} %param.11) | copy-start | bytes 3145732
  23.9 24.2 %all-to-all-start = ((f32[4,1,98304]{2,1,0:T(1,128)}), f32[4,1,98304]{2,1,0:T(1,128)S(1)}, u32[]{:S(2)}, u32[]{:S(2)}) async-start(f32[4,1,98304]{2,1,0:T(1,128)} %reshape.176), calls=%async_computation | async-start | bytes 3145728 | tf_op jit(solution)/shard_map/all_to_all | solution.py:147
  29.8 1.1 copy-start.10
  29.8 1.1 copy-start.12
  29.8 2.2 %copy-start.11 = (s32[16,256]{1,0:T(8,128)S(1)}, s32[16,256]{1,0:T(8,128)}, u32[]{:S(2)}) copy-start(s32[16,256]{1,0:T(8,128)} %param.19) | copy-start | bytes 49156
  48.1 1.2 copy-start.1
  75.9 17.5 %all-to-all-start.1 = ((f32[2,32,16,256]{3,2,0,1:T(8,128)}), f32[2,32,16,256]{3,2,0,1:T(8,128)}, u32[]{:S(2)}, u32[]{:S(2)}) async-start(f32[2,32,16,256]{3,2,0,1:T(8,128)} %copy.59), calls=%async_computation.1 | async-start | bytes 2097152 | tf_op jit(solution)/shard_map/all_to_all | solution.py:149
  85.2 20.7 %copy-start.8 = (f32[16,1024]{1,0:T(8,128)S(1)}, f32[16,1024]{1,0:T(8,128)}, u32[]{:S(2)}) copy-start(f32[16,1024]{1,0:T(8,128)} %param.16) | copy-start | bytes 196612
  85.2 20.8 %copy-start.9 = (f32[16,1024]{1,0:T(8,128)S(1)}, f32[16,1024]{1,0:T(8,128)}, u32[]{:S(2)}) copy-start(f32[16,1024]{1,0:T(8,128)} %param.14) | copy-start | bytes 196612
  93.4 58.9 %all-to-all-start.2 = ((f32[16,256,128]{2,0,1:T(8,128)}), f32[16,256,128]{2,0,1:T(8,128)}, u32[]{:S(2)}, u32[]{:S(2)}) async-start(f32[16,256,128]{2,0,1:T(8,128)} %multiply_bitcast_fusion), calls=%async_computation.2 | async-start | bytes 4194304 | tf_op jit(solution)/shard_map/all_to_all | solution.py:109
  103.0 99.9 %reduce-scatter.2.cloned.1.call-start = ((), (), s32[]{:S(2)}) async-start(), calls=%async_computation.4 | async-start | bytes 655360 | tf_op jit(solution)/shard_map/reduce_scatter | solution.py:158
  155.8 1.4 copy-start
  155.8 1.4 copy-start.7
  157.5 3.8 %collective-permute-start.1 = (f32[34,1,1024]{2,1,0:T(1,128)S(1)}, f32[34,1,1024]{2,1,0:T(1,128)S(1)}, u32[]{:S(2)}, u32[]{:S(2)}) collective-permute-start(f32[34,1,1024]{2,1,0:T(1,128)S(1)} %get-tuple-element.84), channel_id=1, source_target_pairs={{0,16},{16,32},{32,48},{48,64},{64,80},{80,96},{96,112},{112,128},... | collective-permute-start | bytes 417800 | tf_op jit(solution)/shard_map/ppermute | solution.py:19
  159.6 3.3 %collective-permute-start = (f32[34,1,1024]{2,1,0:T(1,128)S(1)}, f32[34,1,1024]{2,1,0:T(1,128)S(1)}, u32[]{:S(2)}, u32[]{:S(2)}) collective-permute-start(f32[34,1,1024]{2,1,0:T(1,128)S(1)} %get-tuple-element.83), channel_id=1, source_target_pairs={{16,0},{32,16},{48,32},{64,48},{80,64},{96,80},{112,96},{128,112},... | collective-permute-start | bytes 417800 | tf_op jit(solution)/shard_map/ppermute | solution.py:21
  163.6 8.6 %copy-start.6 = (f32[16,16,1023]{2,1,0:T(8,128)S(1)}, f32[16,16,1023]{2,1,0:T(8,128)}, u32[]{:S(2)}) copy-start(f32[16,16,1023]{2,1,0:T(8,128)} %get-tuple-element.96) | copy-start | bytes 3142660
  165.3 6.9 %copy-start.5 = (f32[16,16,1023]{2,1,0:T(8,128)S(1)}, f32[16,16,1023]{2,1,0:T(8,128)}, u32[]{:S(2)}) copy-start(f32[16,16,1023]{2,1,0:T(8,128)} %get-tuple-element.95) | copy-start | bytes 3142660
  165.4 10.7 %collective-permute-start.3 = (f32[17,1,1024]{2,1,0:T(1,128)S(1)}, f32[17,1,1024]{2,1,0:T(1,128)S(1)}, u32[]{:S(2)}, u32[]{:S(2)}) collective-permute-start(f32[17,1,1024]{2,1,0:T(1,128)S(1)} %get-tuple-element.88), channel_id=1, source_target_pairs={{0,16},{16,32},{32,48},{48,64},{64,80},{80,96},{96,112},{112,128},... | collective-permute-start | bytes 208904 | tf_op jit(solution)/shard_map/ppermute | solution.py:19
  170.7 5.7 %collective-permute-start.2 = (f32[17,1,1024]{2,1,0:T(1,128)S(1)}, f32[17,1,1024]{2,1,0:T(1,128)S(1)}, u32[]{:S(2)}, u32[]{:S(2)}) collective-permute-start(f32[17,1,1024]{2,1,0:T(1,128)S(1)} %get-tuple-element.87), channel_id=1, source_target_pairs={{16,0},{32,16},{48,32},{64,48},{80,64},{96,80},{112,96},{128,112},... | collective-permute-start | bytes 208904 | tf_op jit(solution)/shard_map/ppermute | solution.py:21
  176.1 1.2 copy-start.3
  176.1 1.5 copy-start.4
  178.4 4.7 %collective-permute-start.5 = (f32[17,1,1024]{2,1,0:T(1,128)S(1)}, f32[17,1,1024]{2,1,0:T(1,128)S(1)}, u32[]{:S(2)}, u32[]{:S(2)}) collective-permute-start(f32[17,1,1024]{2,1,0:T(1,128)S(1)} %get-tuple-element.86), channel_id=1, source_target_pairs={{0,16},{16,32},{32,48},{48,64},{64,80},{80,96},{96,112},{112,128},... | collective-permute-start | bytes 208904 | tf_op jit(solution)/shard_map/ppermute | solution.py:19
  181.8 3.9 %collective-permute-start.4 = (f32[17,1,1024]{2,1,0:T(1,128)S(1)}, f32[17,1,1024]{2,1,0:T(1,128)S(1)}, u32[]{:S(2)}, u32[]{:S(2)}) collective-permute-start(f32[17,1,1024]{2,1,0:T(1,128)S(1)} %get-tuple-element.85), channel_id=1, source_target_pairs={{16,0},{32,16},{48,32},{64,48},{80,64},{96,80},{112,96},{128,112},... | collective-permute-start | bytes 208904 | tf_op jit(solution)/shard_map/ppermute | solution.py:21
Sparse Core Ops, SparseCore 0:
  176.2 26.7 reduce-scatter.1
where the time goes:
time: 211 us; the launch traced here: 210 us
  waiting for transfers between devices  81.3 us (39%)
  local copies, waits for them, and re-layouts  49.5 us (23%)
  starting transfers between devices  35.7 us (17%)
  other arithmetic  24.7 us (12%)
  between operations  14.8 us (7%)
  matrix products  3.79 us (2%)
    all_to_all x1, waiting for transfers between devices, deliver(): lax.all_to_all(packed, 'tile', split_axis=1, concat_axis=1, tiled=True)  40.2 us
    unnamed x43, local copies, waits for them, and re-layouts  19.7 us
    reduce_scatter x1, waiting for transfers between devices, shards(): lax.psum_scatter(jnp.sum(parent_adjoint, axis=0), 'tag', scatter_dimensio...  15.6 us
    all_to_all x1, waiting for transfers between devices, shards(): lax.all_to_all(stacked, 'lev', split_axis=3, concat_axis=1, tiled=True)  13.4 us
    ppermute x3, starting transfers between devices, extended(): lax.ppermute(tail, axis, [(i, (i + 1) % count) for i in range(ends)])  10.3 us
    all_to_all x1, starting transfers between devices, deliver(): lax.all_to_all(packed, 'tile', split_axis=1, concat_axis=1, tiled=True)  9.61 us
    all_to_all x2, local copies, waits for them, and re-layouts, shards(): lax.all_to_all(stacked, 'lev', split_axis=3, concat_axis=1, tiled=True)  8.35 us
    all_to_all x1, waiting for transfers between devices, shards(): lax.all_to_all(column_result, 'lev', split_axis=1, concat_axis=3, tiled=T...  8.27 us
  transfers between devices with their start and end apart: 10, of which 6 were waited for; matrix products, arithmetic and copies ran while one was open for 12% of the time, Pallas kernels for 0%

commit v1 on v0

--- a/solution.py
+++ b/solution.py
@@ -144,7 +144,19 @@
     tag_count = parent_field.shape[0]
     forcing = deliver(parent_field, strip_tile, strip_block, strip_target, strip_count)
     stacked = jnp.concatenate([parent_field, parent_mixing[None]], axis=0)
-    columns = lax.all_to_all(stacked, "lev", split_axis=3, concat_axis=1, tiled=True)
+    ways, here = (lax.axis_size("lev"), lax.axis_index("lev"))
+    width_2 = stacked.shape[3] // ways
+    shape = list(stacked.shape)
+    shape[3] = width_2
+    height = shape[1]
+    shape[1] = height * ways
+    full = jnp.zeros(shape, stacked.dtype)
+    for mask in range(ways):
+        part = lax.dynamic_slice_in_dim(stacked, (here ^ mask) * width_2, width_2, axis=3)
+        if mask:
+            part = lax.ppermute(part, "lev", [(d, d ^ mask) for d in range(ways)])
+        full = lax.dynamic_update_slice_in_dim(full, part, (here ^ mask) * height, axis=1)
+    columns = full
     column_result = tridiagonal(columns[:tag_count], columns[tag_count])
     solved = lax.all_to_all(column_result, "lev", split_axis=1, concat_axis=3, tiled=True)
     parent_adjoint, nest_adjoint = advance(

time: 211 us -> 189 us (0.90)
  local copies, waits for them, and re-layouts: 49.5 us -> 34.3 us
  waiting for transfers between devices: 81.3 us -> 71.7 us
  other arithmetic: 24.7 us -> 31.2 us
  starting transfers between devices: 35.7 us -> 33.1 us
    all_to_all x1 -> x0, waiting for transfers between devices: 13.4 us -> none  [shards(): lax.all_to_all(stacked, 'lev', split_axis=3, concat_axis=1, tiled=True)]
    unnamed x16, other arithmetic: 0.53 us -> 10.5 us
    all_to_all x2 -> x0, local copies, waits for them, and re-layouts: 8.35 us -> none  [shards(): lax.all_to_all(stacked, 'lev', split_axis=3, concat_axis=1, tiled=True)]
    ppermute x0 -> x3, waiting for transfers between devices: none -> 7.98 us  [shards(): part = lax.ppermute(part, 'lev', [(d, d ^ mask) for d in range(ways)])]
    unnamed x43 -> x49, local copies, waits for them, and re-layouts: 19.7 us -> 12.7 us
    concatenate x1 -> x0, local copies, waits for them, and re-layouts: 6.92 us -> none  [shards(): stacked = jnp.concatenate([parent_field, parent_mixing[None]], axis=0)]
    all_to_all x1 -> x0, other arithmetic: 6.16 us -> none  [shards(): lax.all_to_all(stacked, 'lev', split_axis=3, concat_axis=1, tiled=True)]
    all_to_all x1 -> x0, starting transfers between devices: 5.93 us -> none  [shards(): lax.all_to_all(stacked, 'lev', split_axis=3, concat_axis=1, tiled=True)]
  transfers between devices with their start and end apart: 10 -> 12, of which waited for: 6 -> 7; matrix products, arithmetic and copies ran while one was open for 12% -> 18% of each run, Pallas kernels for 0% -> 0%
where the time goes in v1:
time: 189 us; the launch traced here: 188 us
  waiting for transfers between devices  71.7 us (38%)
  local copies, waits for them, and re-layouts  34.3 us (18%)
  starting transfers between devices  33.1 us (18%)
  other arithmetic  31.2 us (17%)
  between operations  14.6 us (8%)
  matrix products  3.2 us (2%)
    all_to_all x1, waiting for transfers between devices, deliver(): lax.all_to_all(packed, 'tile', split_axis=1, concat_axis=1, tiled=True)  38 us
    reduce_scatter x1, waiting for transfers between devices, shards(): lax.psum_scatter(jnp.sum(parent_adjoint, axis=0), 'tag', scatter_dimensio...  15.6 us
    unnamed x49, local copies, waits for them, and re-layouts  12.7 us
    unnamed x16, other arithmetic  10.5 us
    ppermute x3, starting transfers between devices, extended(): lax.ppermute(tail, axis, [(i, (i + 1) % count) for i in range(ends)])  10.4 us
    all_to_all x1, starting transfers between devices, deliver(): lax.all_to_all(packed, 'tile', split_axis=1, concat_axis=1, tiled=True)  8.57 us
    ppermute x3, waiting for transfers between devices, shards(): part = lax.ppermute(part, 'lev', [(d, d ^ mask) for d in range(ways)])  7.98 us
    all_to_all x1, starting transfers between devices, shards(): lax.all_to_all(column_result, 'lev', split_axis=1, concat_axis=3, tiled=T...  6.5 us
  transfers between devices with their start and end apart: 12, of which 7 were waited for; matrix products, arithmetic and copies ran while one was open for 18% of the time, Pallas kernels for 0%

profile of v1, /device:TPU:2, one launch (start us, length us, event | category | flops | bytes accessed | tf_op | source)
XLA Modules:
  0.0 188.2 jit_solution(9808596055891404108)
XLA Ops:
  7.4 0.8 copy-done.9
  8.6 1.1 fusion.41
  9.6 2.3 %collective-permute-start = (f32[3,8,16,256]{3,2,0,1:T(8,128)}, f32[3,8,16,256]{3,2,0,1:T(8,128)}, u32[]{:S(2)}, u32[]{:S(2)}) collective-permute-start(f32[3,8,16,256]{3,2,0,1:T(8,128)} %get-tuple-element.136), channel_id=1, source_target_pairs={{0,4},{4,0},{8,12},{12,8},{1,5},{5,1},{9,13},{13,9},{2,6},{6,2},{1... | collective-permute-start | bytes 1179656 | tf_op jit(solution)/shard_map/ppermute | solution.py:157
  11.9 0.7 collective-permute-start.1
  12.6 0.8 collective-permute-start.2
  13.4 0.7 copy_bitcast_fusion.1
  15.0 0.7 fusion.123
  15.7 1.1 reshape.2623
  17.5 0.7 reshape.2624
  18.1 0.7 reshape.2622
  18.8 1.8 copy.107
  20.6 0.7 convert_element_type.43
  21.3 1.0 collective-permute-done
  22.2 1.0 constant_dynamic-update-slice_fusion.34
  23.3 7.0 %collective-permute-done.1 = f32[3,8,16,256]{3,2,0,1:T(8,128)} collective-permute-done((f32[3,8,16,256]{3,2,0,1:T(8,128)}, f32[3,8,16,256]{3,2,0,1:T(8,128)}, u32[]{:S(2)}, u32[]{:S(2)}) %collective-permute-start.1) | collective-permute-done | bytes 393248 | tf_op jit(solution)/shard_map/ppermute | solution.py:157
  30.3 1.0 constant_dynamic-update-slice_fusion.33
  32.1 1.2 constant_dynamic-update-slice_fusion.31
  52.5 6.5 %all-to-all-start = ((f32[2,32,16,256]{3,2,0,1:T(8,128)}), f32[2,32,16,256]{3,2,0,1:T(8,128)S(1)}, u32[]{:S(2)}, u32[]{:S(2)}) async-start(f32[2,32,16,256]{3,2,0,1:T(8,128)} %constant_dynamic-update-slice_fusion), calls=%async_computation | async-start | bytes 2097152 | tf_op jit(solution)/shard_map/all_to_all | solution.py:161
  59.0 2.4 %gather_fusion = f32[256,16,128]{2,1,0:T(8,128)} fusion(f32[16,128,128]{2,0,1:T(8,128)S(1)} %copy.107, s32[1024]{0:T(1024)S(1)} %pad_clamp_fusion), kind=kCustom, calls=%fused_computation | custom fusion | bytes 4195328 | tf_op jit(solution)/shard_map/jit(_take)/gather | solution.py:108
  61.4 3.7 %multiply_bitcast_fusion = f32[16,256,128]{2,0,1:T(8,128)} fusion(f32[256,16,128]{2,1,0:T(8,128)} %gather_fusion, f32[256]{0:T(256)S(1)} %copy-done.13, pred[256]{0:T(512)(128)(4,1)S(1)} %compare_and_fusion), kind=kLoop, calls=%fused_computation.9 | loop fusion | flops 1048576 | bytes 4195584 | tf_op jit(solution)/shard_map/mul | solution.py:108
  65.1 6.3 %all-to-all-done = f32[2,32,16,256]{3,2,0,1:T(8,128)S(1)} async-done(((f32[2,32,16,256]{3,2,0,1:T(8,128)}), f32[2,32,16,256]{3,2,0,1:T(8,128)S(1)}, u32[]{:S(2)}, u32[]{:S(2)}) %all-to-all-start) | async-done | bytes 1048608 | tf_op jit(solution)/shard_map/all_to_all | solution.py:161
  71.4 1.0 copy-done.2
  72.4 8.6 %all-to-all-start.1 = ((f32[16,256,128]{2,0,1:T(8,128)}), f32[16,256,128]{2,0,1:T(8,128)S(1)}, u32[]{:S(2)}, u32[]{:S(2)}) async-start(f32[16,256,128]{2,0,1:T(8,128)} %multiply_bitcast_fusion), calls=%async_computation.1 | async-start | bytes 4194304 | tf_op jit(solution)/shard_map/all_to_all | solution.py:109
  81.6 0.7 compare_convert_fusion.1
  82.3 0.7 constant_dynamic-slice_fusion
  84.0 0.7 fusion.126
  85.8 2.9 %copy.103 = f32[2,8,16,4,256]{4,3,2,1,0:T(4,128)} copy(f32[2,8,16,4,256]{4,2,0,1,3:T(8,128)} %bitcast.738) | data formatting | bytes 2097152 | tf_op jit(solution)/shard_map/all_to_all | solution.py:161
  88.7 1.8 reshape.2618
  90.5 1.7 fusion.177
  92.2 38.0 %all-to-all-done.1 = f32[16,256,128]{2,0,1:T(8,128)S(1)} async-done(((f32[16,256,128]{2,0,1:T(8,128)}), f32[16,256,128]{2,0,1:T(8,128)S(1)}, u32[]{:S(2)}, u32[]{:S(2)}) %all-to-all-start.1) | async-done | bytes 2097184 | tf_op jit(solution)/shard_map/all_to_all | solution.py:109
  130.2 2.8 %fusion.4 = f32[16,128,128]{2,1,0:T(8,128)} fusion(f32[256,128,1]{0,1,2:T(8,128)S(1)} %convolution_bitcast_fusion, f32[16,256,128]{2,0,1:T(8,128)S(1)} %all-to-all-done.1), kind=kOutput, calls=%fused_computation.19 | convolution fusion | flops 805306368 | bytes 3276800 | tf_op jit(solution)/shard_map/lic,ib->lbc/dot_general | solution.py:127
  133.0 1.4 reshape.2625
  134.4 1.4 add.2478
  136.0 2.3 %collective-permute-start.4 = (f32[34,1,1024]{2,1,0:T(1,128)S(1)}, f32[34,1,1024]{2,1,0:T(1,128)S(1)}, u32[]{:S(2)}, u32[]{:S(2)}) collective-permute-start(f32[34,1,1024]{2,1,0:T(1,128)S(1)} %get-tuple-element.84), channel_id=1, source_target_pairs={{0,16},{16,32},{32,48},{48,64},{64,80},{80,96},{96,112},{112,128},... | collective-permute-start | bytes 417800 | tf_op jit(solution)/shard_map/ppermute | solution.py:19
  138.3 1.3 collective-permute-start.3
  140.0 1.5 collective-permute-done.3
  141.6 0.7 fusion.13
  142.4 1.7 fusion.175
  144.1 5.1 %collective-permute-start.6 = (f32[17,1,1024]{2,1,0:T(1,128)S(1)}, f32[17,1,1024]{2,1,0:T(1,128)S(1)}, u32[]{:S(2)}, u32[]{:S(2)}) collective-permute-start(f32[17,1,1024]{2,1,0:T(1,128)S(1)} %get-tuple-element.141), channel_id=1, source_target_pairs={{0,16},{16,32},{32,48},{48,64},{64,80},{80,96},{96,112},{112,128},... | collective-permute-start | bytes 208904 | tf_op jit(solution)/shard_map/ppermute | solution.py:19
  149.2 1.3 collective-permute-start.5
  150.5 1.7 fusion.35
  152.2 2.2 %reduce_sum.39 = f32[8,16,1024]{2,1,0:T(8,128)} reduce(f32[2,8,16,1024]{3,2,1,0:T(8,128)} %bitcast.739, f32[]{:T(128)} %constant.27.clone.1), dimensions={0}, to_apply=%region_7.8 | reduce | flops 131072 | bytes 1572868 | tf_op jit(solution)/shard_map/reduce_sum | solution.py:171
  154.7 0.9 copy-done.3
  156.7 3.0 %collective-permute-start.8 = (f32[17,1,1024]{2,1,0:T(1,128)S(1)}, f32[17,1,1024]{2,1,0:T(1,128)S(1)}, u32[]{:S(2)}, u32[]{:S(2)}) collective-permute-start(f32[17,1,1024]{2,1,0:T(1,128)S(1)} %get-tuple-element.139), channel_id=1, source_target_pairs={{0,16},{16,32},{32,48},{48,64},{64,80},{80,96},{96,112},{112,128},... | collective-permute-start | bytes 208904 | tf_op jit(solution)/shard_map/ppermute | solution.py:19
  160.2 1.3 collective-permute-start.7
  161.8 2.3 %collective-permute-done.7 = f32[17,1,1024]{2,1,0:T(1,128)S(1)} collective-permute-done((f32[17,1,1024]{2,1,0:T(1,128)S(1)}, f32[17,1,1024]{2,1,0:T(1,128)S(1)}, u32[]{:S(2)}, u32[]{:S(2)}) %collective-permute-start.7) | collective-permute-done | bytes 69664 | tf_op jit(solution)/shard_map/ppermute | solution.py:21
  164.1 1.6 fusion.27
  165.7 15.6 %reduce-scatter.2.cloned.1.call-done = f32[8,16,256]{2,1,0:T(8,128)} async-done(((f32[8,16,1024]{2,1,0:T(8,128)}), f32[8,16,256]{2,1,0:T(8,128)}) %reduce-scatter.2.cloned.1.call-update) | async-done | bytes 131088 | tf_op jit(solution)/shard_map/reduce_scatter | solution.py:170
  (126 shorter events, 27.6 us)
Async XLA Ops:
  7.2 1.0 copy-start.9
  7.2 1.4 copy-start.1
  8.6 4.8 %copy-start.11 = (s32[16,256]{1,0:T(8,128)S(1)}, s32[16,256]{1,0:T(8,128)}, u32[]{:S(2)}) copy-start(s32[16,256]{1,0:T(8,128)} %param.18) | copy-start | bytes 49156
  9.6 7.2 %copy-start.12 = (s32[16,256]{1,0:T(8,128)S(1)}, s32[16,256]{1,0:T(8,128)}, u32[]{:S(2)}) copy-start(s32[16,256]{1,0:T(8,128)} %param.19) | copy-start | bytes 49156
  9.6 12.6 %collective-permute-start = (f32[3,8,16,256]{3,2,0,1:T(8,128)}, f32[3,8,16,256]{3,2,0,1:T(8,128)}, u32[]{:S(2)}, u32[]{:S(2)}) collective-permute-start(f32[3,8,16,256]{3,2,0,1:T(8,128)} %get-tuple-element.136), channel_id=1, source_target_pairs={{0,4},{4,0},{8,12},{12,8},{1,5},{5,1},{9,13},{13,9},{2,6},{6,2},{1... | collective-permute-start | bytes 1179656 | tf_op jit(solution)/shard_map/ppermute | solution.py:157
  11.9 18.4 %collective-permute-start.1 = (f32[3,8,16,256]{3,2,0,1:T(8,128)}, f32[3,8,16,256]{3,2,0,1:T(8,128)}, u32[]{:S(2)}, u32[]{:S(2)}) collective-permute-start(f32[3,8,16,256]{3,2,0,1:T(8,128)} %get-tuple-element.137), channel_id=1, source_target_pairs={{0,8},{4,12},{8,0},{12,4},{1,9},{5,13},{9,1},{13,5},{2,10},{6,14},... | collective-permute-start | bytes 1179656 | tf_op jit(solution)/shard_map/ppermute | solution.py:157
  12.6 18.7 %collective-permute-start.2 = (f32[3,8,16,256]{3,2,0,1:T(8,128)S(1)}, f32[3,8,16,256]{3,2,0,1:T(8,128)S(1)}, u32[]{:S(2)}, u32[]{:S(2)}) collective-permute-start(f32[3,8,16,256]{3,2,0,1:T(8,128)S(1)} %get-tuple-element.134), channel_id=1, source_target_pairs={{0,12},{4,8},{8,4},{12,0},{1,13},{5,9},{9,5},{13,1},{2,14},{6,10},... | collective-permute-start | bytes 1179656 | tf_op jit(solution)/shard_map/ppermute | solution.py:157
  46.3 12.7 %copy-start.14 = (s32[256,1]{0,1:T(1,128)S(1)}, s32[256,1]{0,1:T(1,128)}, u32[]{:S(2)}) copy-start(s32[256,1]{0,1:T(1,128)} %reshape.2624) | copy-start | bytes 3076
  52.5 18.9 %all-to-all-start = ((f32[2,32,16,256]{3,2,0,1:T(8,128)}), f32[2,32,16,256]{3,2,0,1:T(8,128)S(1)}, u32[]{:S(2)}, u32[]{:S(2)}) async-start(f32[2,32,16,256]{3,2,0,1:T(8,128)} %constant_dynamic-update-slice_fusion), calls=%async_computation | async-start | bytes 2097152 | tf_op jit(solution)/shard_map/all_to_all | solution.py:161
  59.0 2.4 %copy-start.16 = (s32[256]{0:T(256)S(1)}, s32[256]{0:T(256)}, u32[]{:S(2)}) copy-start(s32[256]{0:T(256)} %reshape.2622) | copy-start | bytes 3076
  59.0 2.4 %copy-start.13 = (f32[256]{0:T(256)S(1)}, f32[256]{0:T(256)}, u32[]{:S(2)}) copy-start(f32[256]{0:T(256)} %convert_element_type.43) | copy-start | bytes 3076
  65.1 15.9 %copy-start.15 = (s32[16]{0:T(128)S(1)}, s32[16]{0:T(128)}, u32[]{:S(2)}) copy-start(s32[16]{0:T(128)} %param.21) | copy-start | bytes 196
  65.1 18.7 %copy-start.10 = (f32[16,1024]{1,0:T(8,128)S(1)}, f32[16,1024]{1,0:T(8,128)}, u32[]{:S(2)}) copy-start(f32[16,1024]{1,0:T(8,128)} %param.14) | copy-start | bytes 196612
  65.1 18.8 %copy-start.8 = (f32[16,1024]{1,0:T(8,128)S(1)}, f32[16,1024]{1,0:T(8,128)}, u32[]{:S(2)}) copy-start(f32[16,1024]{1,0:T(8,128)} %param.16) | copy-start | bytes 196612
  71.4 1.0 copy-start.2
  72.4 57.8 %all-to-all-start.1 = ((f32[16,256,128]{2,0,1:T(8,128)}), f32[16,256,128]{2,0,1:T(8,128)S(1)}, u32[]{:S(2)}, u32[]{:S(2)}) async-start(f32[16,256,128]{2,0,1:T(8,128)} %multiply_bitcast_fusion), calls=%async_computation.1 | async-start | bytes 4194304 | tf_op jit(solution)/shard_map/all_to_all | solution.py:109
  81.0 100.3 %reduce-scatter.2.cloned.1.call-start = ((), (), s32[]{:S(2)}) async-start(), calls=%async_computation.3 | async-start | bytes 655360 | tf_op jit(solution)/shard_map/reduce_scatter | solution.py:170
  134.3 1.4 copy-start
  134.4 1.4 copy-start.7
  136.0 4.0 %collective-permute-start.4 = (f32[34,1,1024]{2,1,0:T(1,128)S(1)}, f32[34,1,1024]{2,1,0:T(1,128)S(1)}, u32[]{:S(2)}, u32[]{:S(2)}) collective-permute-start(f32[34,1,1024]{2,1,0:T(1,128)S(1)} %get-tuple-element.84), channel_id=1, source_target_pairs={{0,16},{16,32},{32,48},{48,64},{64,80},{80,96},{96,112},{112,128},... | collective-permute-start | bytes 417800 | tf_op jit(solution)/shard_map/ppermute | solution.py:19
  138.3 3.3 %collective-permute-start.3 = (f32[34,1,1024]{2,1,0:T(1,128)S(1)}, f32[34,1,1024]{2,1,0:T(1,128)S(1)}, u32[]{:S(2)}, u32[]{:S(2)}) collective-permute-start(f32[34,1,1024]{2,1,0:T(1,128)S(1)} %get-tuple-element.83), channel_id=1, source_target_pairs={{16,0},{32,16},{48,32},{64,48},{80,64},{96,80},{112,96},{128,112},... | collective-permute-start | bytes 417800 | tf_op jit(solution)/shard_map/ppermute | solution.py:21
  142.4 8.1 %copy-start.5 = (f32[16,16,1023]{2,1,0:T(8,128)S(1)}, f32[16,16,1023]{2,1,0:T(8,128)}, u32[]{:S(2)}) copy-start(f32[16,16,1023]{2,1,0:T(8,128)} %get-tuple-element.148) | copy-start | bytes 3142660
  142.4 8.1 %copy-start.6 = (f32[16,16,1023]{2,1,0:T(8,128)S(1)}, f32[16,16,1023]{2,1,0:T(8,128)}, u32[]{:S(2)}) copy-start(f32[16,16,1023]{2,1,0:T(8,128)} %get-tuple-element.149) | copy-start | bytes 3142660
  144.1 10.3 %collective-permute-start.6 = (f32[17,1,1024]{2,1,0:T(1,128)S(1)}, f32[17,1,1024]{2,1,0:T(1,128)S(1)}, u32[]{:S(2)}, u32[]{:S(2)}) collective-permute-start(f32[17,1,1024]{2,1,0:T(1,128)S(1)} %get-tuple-element.141), channel_id=1, source_target_pairs={{0,16},{16,32},{32,48},{48,64},{64,80},{80,96},{96,112},{112,128},... | collective-permute-start | bytes 208904 | tf_op jit(solution)/shard_map/ppermute | solution.py:19
  149.2 5.5 %collective-permute-start.5 = (f32[17,1,1024]{2,1,0:T(1,128)S(1)}, f32[17,1,1024]{2,1,0:T(1,128)S(1)}, u32[]{:S(2)}, u32[]{:S(2)}) collective-permute-start(f32[17,1,1024]{2,1,0:T(1,128)S(1)} %get-tuple-element.140), channel_id=1, source_target_pairs={{16,0},{32,16},{48,32},{64,48},{80,64},{96,80},{112,96},{128,112},... | collective-permute-start | bytes 208904 | tf_op jit(solution)/shard_map/ppermute | solution.py:21
  154.4 1.2 copy-start.3
  154.4 1.5 copy-start.4
  156.7 4.7 %collective-permute-start.8 = (f32[17,1,1024]{2,1,0:T(1,128)S(1)}, f32[17,1,1024]{2,1,0:T(1,128)S(1)}, u32[]{:S(2)}, u32[]{:S(2)}) collective-permute-start(f32[17,1,1024]{2,1,0:T(1,128)S(1)} %get-tuple-element.139), channel_id=1, source_target_pairs={{0,16},{16,32},{32,48},{48,64},{64,80},{80,96},{96,112},{112,128},... | collective-permute-start | bytes 208904 | tf_op jit(solution)/shard_map/ppermute | solution.py:19
  160.2 3.9 %collective-permute-start.7 = (f32[17,1,1024]{2,1,0:T(1,128)S(1)}, f32[17,1,1024]{2,1,0:T(1,128)S(1)}, u32[]{:S(2)}, u32[]{:S(2)}) collective-permute-start(f32[17,1,1024]{2,1,0:T(1,128)S(1)} %get-tuple-element.138), channel_id=1, source_target_pairs={{16,0},{32,16},{48,32},{64,48},{80,64},{96,80},{112,96},{128,112},... | collective-permute-start | bytes 208904 | tf_op jit(solution)/shard_map/ppermute | solution.py:21
Sparse Core Ops, SparseCore 0:
  154.6 26.7 reduce-scatter.1
